TPU v7x, 512 devices: a whole 4x8x8 slice. The times are simulated.
512 devices in a mesh: owner: 64 (over z, x, core), col: 8 (over y).
Axes of the slice: x: 4, y: 8, z: 8, core: 2. Of those that a mesh axis runs over, the one named last changes fastest.
Arguments:
- ks_tiles: bfloat16 [8192, 128, 128], P(('owner', 'col')), may hold values from -0.21875 to 0.21875
- chem_shift: float32 [1], replicated, may hold values from -0.4 to 0.4
- spectral_scale: float32 [1], replicated, may hold values from 1.25 to 2
- sub_tiles: int32 [512, 6, 6], replicated, may hold values from -1 to 8191, as said below
- result_dest: int32 [512, 6], replicated, may hold values from -1 to 8191, as said below
Outputs:
- density_tiles: float32 [8192, 128, 128], P(('owner', 'col'))
- electrons: float32 [1], replicated
Inputs may be any that keep to these rules, and one draw needn't show every extreme that they name: `sub_tiles`: -1 marks a zero block. An entry t names a tile held by the device of mesh index t // 16 (owner index times the number of col devices plus col index); that owner index differs from the owner index of device s by at most one, cyclically. At most 2 entries of one submatrix name tiles of one device, and in every submatrix some device holds exactly 2 of its nonzero blocks. `result_dest`: -1 drops the block. An entry t names a tile of a device with the col index of device s and an owner index that differs from that of device s by at most one, cyclically. At most 3 entries of one submatrix go to one device, and every submatrix sends exactly 3 to some device. Blocks sent to the same tile are added.
All inputs are finite; a program needn't handle non-finite values.
Results may differ from a plain program's by a relative error of at most 0.0003.
Values may be sent and summed in bfloat16 or wider, within the bound.
A program may use at most 64 MiB of HBM per device.

v0:
```python
import jax
import jax.numpy as jnp
from jax import lax
from jax.sharding import PartitionSpec as P

ITERS = 2


def with_halo(block, sides, width):
    for axis, dim in sides:
        count = lax.axis_size(axis)
        forward = [(i, i + 1) for i in range(count - 1)]
        forward.append((count - 1, 0))
        backward = [(target, source) for source, target in forward]
        low = lax.ppermute(
            lax.slice_in_dim(block, block.shape[dim] - width, None, axis=dim), axis, forward
        )
        high = lax.ppermute(lax.slice_in_dim(block, 0, width, axis=dim), axis, backward)
        block = jnp.concatenate([low, block, high], axis=dim)
    return block


def sign_density(tile_block, chem_shift, spectral_scale):
    blocks = tile_block.shape[0]
    edge_len = tile_block.shape[2]
    matrix_order = blocks * edge_len
    assembled = jnp.transpose(tile_block, (0, 2, 1, 3)).reshape(matrix_order, matrix_order)
    identity = jnp.eye(matrix_order, dtype=assembled.dtype)
    current = (0.5 * (assembled + assembled.T) - chem_shift[0] * identity) / spectral_scale[0]
    for sweep in range(ITERS):
        square = jnp.dot(
            current, current, precision=lax.Precision.HIGHEST, preferred_element_type=jnp.float32
        )
        cube_term = jnp.dot(
            current, square, precision=lax.Precision.HIGHEST, preferred_element_type=jnp.float32
        )
        current = 1.5 * current - 0.5 * cube_term
    return 0.5 * (identity - current)


def source_ranks(tile_lists, tiles_per):
    usable = tile_lists >= 0
    device = jnp.where(usable, tile_lists // tiles_per, -1)
    positions = tile_lists.shape[-1]
    earlier = jnp.arange(positions)[:, None] > jnp.arange(positions)[None, :]
    shared = (device[..., :, None] == device[..., None, :]) & usable[..., None, :] & earlier
    return (device, jnp.sum(shared.astype(jnp.int32), axis=-1))


def owner_ranks(destinations, tiles_per, columns):
    usable = destinations >= 0
    to_owner = jnp.where(usable, destinations // tiles_per // columns, -1)
    positions = destinations.shape[-1]
    earlier = jnp.arange(positions)[:, None] > jnp.arange(positions)[None, :]
    shared = (to_owner[..., :, None] == to_owner[..., None, :]) & usable[..., None, :] & earlier
    return (to_owner, jnp.sum(shared.astype(jnp.int32), axis=-1), usable)


def on_device(ks_tiles, chem_shift, spectral_scale, sub_tiles, result_dest):
    owners = lax.axis_size("owner")
    columns = lax.axis_size("col")
    tiles_per = ks_tiles.shape[0]
    edge_len = ks_tiles.shape[1]
    blocks = sub_tiles.shape[1]
    positions = blocks * blocks
    capacity = max(2, (positions + 3 * columns - 1) // (3 * columns))
    room_back = blocks // 2
    owner_at = lax.axis_index("owner")
    column_at = lax.axis_index("col")
    myself = owner_at * columns + column_at
    offsets = jnp.arange(3, dtype=jnp.int32) - 1
    near_owner = (owner_at + offsets + owners) % owners
    lists_flat = sub_tiles.reshape(sub_tiles.shape[0], positions)
    receivers = near_owner[:, None] * columns + jnp.arange(columns, dtype=jnp.int32)[None, :]
    wanted = jnp.take(lists_flat, receivers, axis=0)
    device, ranking = source_ranks(wanted, tiles_per)
    matches = (device == myself)[..., None] & (
        ranking[..., None] == jnp.arange(capacity)[None, None, None, :]
    )
    local_slot = jnp.sum(jnp.where(matches, (wanted % tiles_per)[..., None], 0), axis=2)
    packet = jnp.take(ks_tiles, local_slot.reshape(-1), axis=0).reshape(
        3, columns, capacity, edge_len, edge_len
    )
    near_in = with_halo(jnp.stack([packet[0], packet[2]]), (("owner", 0),), 1)
    sectioned = jnp.stack([near_in[0], packet[1], near_in[3]])
    arrived = lax.all_to_all(sectioned, "col", split_axis=1, concat_axis=1, tiled=True)
    own_list = lax.dynamic_index_in_dim(lists_flat, myself, 0, keepdims=False)
    own_device, own_rank = source_ranks(own_list, tiles_per)
    relative = (own_device // columns - owner_at + owners + 1) % owners
    present = own_list >= 0
    position = jnp.where(
        present, (relative * columns + own_device % columns) * capacity + own_rank, 0
    )
    picked = jnp.take(arrived.reshape(-1, edge_len, edge_len), position, axis=0)
    tile_block = jnp.where(present[:, None, None], picked.astype(jnp.float32), 0.0)
    tile_block = tile_block.reshape(blocks, blocks, edge_len, edge_len)
    density = sign_density(tile_block, chem_shift, spectral_scale)
    result_cols = density[:, :edge_len].reshape(blocks, edge_len, edge_len)
    summed = lax.psum(jnp.trace(density[:edge_len, :edge_len]), ("owner", "col"))
    electrons = (2.0 * summed).reshape(1)
    own_dest = lax.dynamic_index_in_dim(result_dest, myself, 0, keepdims=False)
    to_owner, back_rank, usable = owner_ranks(own_dest, tiles_per, columns)
    toward = (to_owner - owner_at + owners + 1) % owners
    select = usable[None, None, :] & (toward[None, None, :] == jnp.arange(3)[:, None, None])
    select = select & (back_rank[None, None, :] == jnp.arange(room_back)[None, :, None])
    outgoing = jnp.einsum(
        "dki,ixy->dkxy", select.astype(jnp.float32), result_cols, precision=lax.Precision.HIGHEST
    )
    back_in = with_halo(jnp.stack([outgoing[0], outgoing[2]]), (("owner", 0),), 1)
    returned = jnp.stack([back_in[0], outgoing[1], back_in[3]])
    senders = near_owner * columns + column_at
    sent_dest = jnp.take(result_dest, senders, axis=0)
    sent_owner, sent_rank, sent_usable = owner_ranks(sent_dest, tiles_per, columns)
    to_me = sent_usable & (sent_owner == owner_at)
    position_back = jnp.where(to_me, jnp.arange(3)[:, None] * room_back + sent_rank, 0)
    pieces = jnp.take(
        returned.reshape(3 * room_back, edge_len * edge_len), position_back.reshape(-1), axis=0
    )
    store_match = (sent_dest % tiles_per).reshape(-1)[None, :] == jnp.arange(tiles_per)[:, None]
    weights = (to_me.reshape(-1)[None, :] & store_match).astype(jnp.float32)
    density_tiles = jnp.dot(
        weights, pieces, precision=lax.Precision.HIGHEST, preferred_element_type=jnp.float32
    )
    density_tiles = density_tiles.reshape(tiles_per, edge_len, edge_len)
    return (density_tiles, electrons)


def solution(mesh):
    return jax.shard_map(
        on_device,
        mesh=mesh,
        in_specs=(P(("owner", "col"), None, None), P(), P(), P(), P()),
        out_specs=(P(("owner", "col"), None, None), P()),
        check_vma=False,
    )
```

profile of v0, /device:TPU:1, one launch (start us, length us, event | category | flops | bytes accessed | tf_op | source)
XLA Modules:
  0.0 221.3 jit_solution(15316499976088127040)
XLA Ops:
  0.9 0.9 reshape.1038
  2.8 2.0 convert_reduce_fusion
  5.5 0.8 gather_fusion.2
  6.7 4.5 %collective-permute-start = (bf16[1,8,2,128,128]{4,3,2,0,1:T(8,128)(2,1)S(1)}, bf16[1,8,2,128,128]{4,3,2,0,1:T(8,128)(2,1)S(1)}, u32[]{:S(2)}, u32[]{:S(2)}) collective-permute-start(bf16[1,8,2,128,128]{4,3,2,0,1:T(8,128)(2,1)S(1)} %bitcast.126), channel_id=1, source_target_pairs={{0,8},{8,16},{16,24},{24,32},{32,40},{40,48},{48,56},{56,64},{64,7... | collective-permute-start | bytes 1572872 | tf_op jit(solution)/shard_map/ppermute | solution.py:15
  11.2 6.2 %collective-permute-start.1 = (bf16[1,8,2,128,128]{4,3,2,0,1:T(8,128)(2,1)S(1)}, bf16[1,8,2,128,128]{4,3,2,0,1:T(8,128)(2,1)S(1)}, u32[]{:S(2)}, u32[]{:S(2)}) collective-permute-start(bf16[1,8,2,128,128]{4,3,2,0,1:T(8,128)(2,1)S(1)} %bitcast.125), channel_id=1, source_target_pairs={{8,0},{16,8},{24,16},{32,24},{40,32},{48,40},{56,48},{64,56},{72,6... | collective-permute-start | bytes 1572872 | tf_op jit(solution)/shard_map/ppermute | solution.py:18
  18.6 3.4 %collective-permute-done.1 = bf16[1,8,2,128,128]{4,3,2,0,1:T(8,128)(2,1)S(1)} collective-permute-done((bf16[1,8,2,128,128]{4,3,2,0,1:T(8,128)(2,1)S(1)}, bf16[1,8,2,128,128]{4,3,2,0,1:T(8,128)(2,1)S(1)}, u32[]{:S(2)}, u32[]{:S(2)}) %collective-permute-start.1) | collective-permute-done | bytes 524320 | tf_op jit(solution)/shard_map/ppermute | solution.py:18
  22.0 1.3 pad_maximum_fusion
  23.3 6.8 %all-to-all-start = ((bf16[3,8,2,128,128]{4,3,2,0,1:T(8,128)(2,1)}), bf16[3,8,2,128,128]{4,3,2,0,1:T(8,128)(2,1)S(1)}, u32[]{:S(2)}, u32[]{:S(2)}) async-start(bf16[3,8,2,128,128]{4,3,2,0,1:T(8,128)(2,1)} %pad_maximum_fusion), calls=%async_computation | async-start | bytes 3145728 | tf_op jit(solution)/shard_map/all_to_all | solution.py:86
  33.3 31.7 %all-to-all-done = bf16[3,8,2,128,128]{4,3,2,0,1:T(8,128)(2,1)S(1)} async-done(((bf16[3,8,2,128,128]{4,3,2,0,1:T(8,128)(2,1)}), bf16[3,8,2,128,128]{4,3,2,0,1:T(8,128)(2,1)S(1)}, u32[]{:S(2)}, u32[]{:S(2)}) %all-to-all-start) | async-done | bytes 1572896 | tf_op jit(solution)/shard_map/all_to_all | solution.py:86
  65.0 1.3 copy.44
  66.3 2.2 gather_fusion.3
  68.8 1.4 copy.45
  70.8 2.0 copy.46
  72.8 8.6 %fusion.74 = f32[768,768]{1,0:T(8,128)S(1)} fusion(f32[768,768]{1,0:T(8,128)S(1)} %bitcast.116, f32[768,768]{0,1:T(8,128)} %copy.46, f32[]{:T(128)} %bitcast.112, f32[]{:T(128)} %bitcast.110), kind=kOutput, calls=%fused_computation.233 | convolution fusion | flops 5439356928 | bytes 7077896 | tf_op jit(solution)/shard_map/dot_general | solution.py:31
  81.4 6.1 %multiply_subtract_fusion = f32[768,768]{1,0:T(8,128)S(1)} fusion(f32[768,768]{1,0:T(8,128)S(1)} %fusion.74, f32[]{:T(128)} %bitcast.111, f32[]{:T(128)} %bitcast.109, f32[768,768]{1,0:T(8,128)S(1)} %bitcast.117, f32[768,768]{0,1:T(8,128)S(1)} %copy-done.1), kind=kOutput, calls=%fused_computation.11 | convolution fusion | flops 5444665344 | bytes 9437192 | tf_op jit(solution)/shard_map/dot_general | solution.py:34
  87.6 6.2 %fusion.83 = f32[768,768]{1,0:T(8,128)S(1)} fusion(f32[768,768]{1,0:T(8,128)S(1)} %multiply_subtract_fusion), kind=kOutput, calls=%fused_computation.238 | convolution fusion | flops 5435817984 | bytes 4718592 | tf_op jit(solution)/shard_map/dot_general | solution.py:31
  93.8 6.2 %subtract_multiply_fusion = f32[768,768]{1,0:T(8,128)S(1)} fusion(f32[768,768]{1,0:T(8,128)S(1)} %multiply_subtract_fusion, f32[768,768]{1,0:T(8,128)S(1)} %fusion.83), kind=kOutput, calls=%fused_computation.10 | convolution fusion | flops 5439946752 | bytes 7077888 | tf_op jit(solution)/shard_map/dot_general | solution.py:34
  100.0 0.9 fusion.10
  101.1 8.2 %collective-permute-start.2 = (f32[1,3,128,128]{3,1,2,0:T(4,128)S(1)}, f32[1,3,128,128]{3,1,2,0:T(4,128)S(1)}, u32[]{:S(2)}, u32[]{:S(2)}) collective-permute-start(f32[1,3,128,128]{3,1,2,0:T(4,128)S(1)} %get-tuple-element.21), channel_id=1, source_target_pairs={{0,8},{8,16},{16,24},{24,32},{32,40},{40,48},{48,56},{56,64},{64,7... | collective-permute-start | bytes 589832 | tf_op jit(solution)/shard_map/ppermute | solution.py:15
  109.3 1.9 collective-permute-start.3
  111.9 103.7 %psum.7 = f32[]{:T(128)} all-reduce(f32[]{:T(128)} %fusion.13), channel_id=1, replica_groups=mesh['owner'=64,'col'=8] {'owner','col'}, use_global_device_ids=true, to_apply=%region_6.7 | all-reduce | flops 1 | bytes 8 | tf_op jit(solution)/shard_map/psum | solution.py:99
  217.2 1.0 gather_fusion.4
  218.2 0.8 fusion.5
  219.0 1.2 copy.52
  (73 shorter events, 7.8 us)
Async XLA Ops:
  0.6 4.8 %copy-start = (bf16[16,128,128]{2,1,0:T(8,128)(2,1)S(1)}, bf16[16,128,128]{2,1,0:T(8,128)(2,1)}, u32[]{:S(2)}) copy-start(bf16[16,128,128]{2,1,0:T(8,128)(2,1)} %param.5) | copy-start | bytes 1572868
  6.6 10.9 %copy-start.2 = (s32[512,6]{0,1:T(8,128)S(1)}, s32[512,6]{0,1:T(8,128)}, u32[]{:S(2)}) copy-start(s32[512,6]{0,1:T(8,128)} %param.9) | copy-start | bytes 36868
  6.7 11.9 %collective-permute-start = (bf16[1,8,2,128,128]{4,3,2,0,1:T(8,128)(2,1)S(1)}, bf16[1,8,2,128,128]{4,3,2,0,1:T(8,128)(2,1)S(1)}, u32[]{:S(2)}, u32[]{:S(2)}) collective-permute-start(bf16[1,8,2,128,128]{4,3,2,0,1:T(8,128)(2,1)S(1)} %bitcast.126), channel_id=1, source_target_pairs={{0,8},{8,16},{16,24},{24,32},{32,40},{40,48},{48,56},{56,64},{64,7... | collective-permute-start | bytes 1572872 | tf_op jit(solution)/shard_map/ppermute | solution.py:15
  11.2 10.8 %collective-permute-start.1 = (bf16[1,8,2,128,128]{4,3,2,0,1:T(8,128)(2,1)S(1)}, bf16[1,8,2,128,128]{4,3,2,0,1:T(8,128)(2,1)S(1)}, u32[]{:S(2)}, u32[]{:S(2)}) collective-permute-start(bf16[1,8,2,128,128]{4,3,2,0,1:T(8,128)(2,1)S(1)} %bitcast.125), channel_id=1, source_target_pairs={{8,0},{16,8},{24,16},{32,24},{40,32},{48,40},{56,48},{64,56},{72,6... | collective-permute-start | bytes 1572872 | tf_op jit(solution)/shard_map/ppermute | solution.py:18
  23.3 41.7 %all-to-all-start = ((bf16[3,8,2,128,128]{4,3,2,0,1:T(8,128)(2,1)}), bf16[3,8,2,128,128]{4,3,2,0,1:T(8,128)(2,1)S(1)}, u32[]{:S(2)}, u32[]{:S(2)}) async-start(bf16[3,8,2,128,128]{4,3,2,0,1:T(8,128)(2,1)} %pad_maximum_fusion), calls=%async_computation | async-start | bytes 3145728 | tf_op jit(solution)/shard_map/all_to_all | solution.py:86
  72.8 8.7 %copy-start.1 = (f32[768,768]{0,1:T(8,128)S(1)}, f32[768,768]{0,1:T(8,128)}, u32[]{:S(2)}) copy-start(f32[768,768]{0,1:T(8,128)} %copy.46) | copy-start | bytes 7077892
  101.1 115.2 %collective-permute-start.2 = (f32[1,3,128,128]{3,1,2,0:T(4,128)S(1)}, f32[1,3,128,128]{3,1,2,0:T(4,128)S(1)}, u32[]{:S(2)}, u32[]{:S(2)}) collective-permute-start(f32[1,3,128,128]{3,1,2,0:T(4,128)S(1)} %get-tuple-element.21), channel_id=1, source_target_pairs={{0,8},{8,16},{16,24},{24,32},{32,40},{40,48},{48,56},{56,64},{64,7... | collective-permute-start | bytes 589832 | tf_op jit(solution)/shard_map/ppermute | solution.py:15
  109.3 106.9 %collective-permute-start.3 = (f32[1,3,128,128]{3,1,2,0:T(4,128)S(1)}, f32[1,3,128,128]{3,1,2,0:T(4,128)S(1)}, u32[]{:S(2)}, u32[]{:S(2)}) collective-permute-start(f32[1,3,128,128]{3,1,2,0:T(4,128)S(1)} %get-tuple-element.22), channel_id=1, source_target_pairs={{8,0},{16,8},{24,16},{32,24},{40,32},{48,40},{56,48},{64,56},{72,6... | collective-permute-start | bytes 589832 | tf_op jit(solution)/shard_map/ppermute | solution.py:18
where the time goes:
time: 222 us; the launch traced here: 221 us
  blocking collectives  104 us (47%)
  waiting for transfers between devices  35.1 us (16%)
  matrix products  28.9 us (13%)
  starting transfers between devices  27.7 us (12%)
  local copies, waits for them, and re-layouts  14.7 us (7%)
  other arithmetic  7.08 us (3%)
  between operations  4.12 us (2%)
    psum x1, blocking collectives, on_device(): lax.psum(jnp.trace(density[:edge_len, :edge_len]), ('owner', 'col'))  104 us
    all_to_all x1, waiting for transfers between devices, on_device(): lax.all_to_all(sectioned, 'col', split_axis=1, concat_axis=1, tiled=True)  31.7 us
    dot_general x2, matrix products, sign_density(): jnp.dot(current, current, precision=lax.Precision.HIGHEST, preferred_elem...  14.8 us
    ppermute x2, starting transfers between devices, with_halo(): lax.ppermute(lax.slice_in_dim(block, block.shape[dim] - width, None, axis...  12.8 us
    dot_general x2, matrix products, sign_density(): jnp.dot(current, square, precision=lax.Precision.HIGHEST, preferred_eleme...  12.3 us
    ppermute x2, starting transfers between devices, with_halo(): lax.ppermute(lax.slice_in_dim(block, 0, width, axis=dim), axis, backward)  8.12 us
    all_to_all x1, starting transfers between devices, on_device(): lax.all_to_all(sectioned, 'col', split_axis=1, concat_axis=1, tiled=True)  6.82 us
  transfers between devices with their start and end apart: 5, of which 2 were waited for; matrix products, arithmetic and copies ran while one was open for 2% of the time, Pallas kernels for 0%

commit v1 on v0

v1 whole, which is shorter than its diff:
```python
import functools
import jax
import jax.numpy as jnp
from jax import lax
from jax.experimental import pallas as pl
from jax.experimental.pallas import tpu as pltpu
from jax.sharding import PartitionSpec as P

F32 = jnp.float32
BF16 = jnp.bfloat16
MESH = pl.DeviceIdType.MESH
ROOM = 2
BACK = 3
FAR = 1 << 20


def log2(n):
    assert n & (n - 1) == 0
    return n.bit_length() - 1


def dot(a, b, contract):
    return lax.dot_general(a, b, (contract, ((), ())), preferred_element_type=F32)


def kernel(
    owners, columns, inner, blocks, chem_ref, scale_ref, tiles_ref, sub_ref, dest_ref,
    out_ref, elec_ref, lists, dests, packet, arrived, place, matrix, results, going, back,
    trace_out, trace_in, list_sem, send_sem, recv_sem, back_send, back_recv, trace_send, trace_recv,
):
    tiles_per, edge = tiles_ref.shape[0], tiles_ref.shape[1]
    outer = owners // inner
    owner = lax.axis_index("owner")
    column = lax.axis_index("col")
    myself = owner * columns + column
    tile_bits, column_bits = log2(tiles_per), log2(columns)
    near = [lax.rem(owner + owners + r - 1, owners) for r in range(3)]
    ring = [lax.rem(column + dy, columns) for dy in range(columns)]
    in_block = lax.rem(owner, inner)
    block_start = owner - in_block
    mates = [block_start + lax.rem(in_block + k, inner) for k in range(inner)]
    across = [lax.rem(owner + k * inner, owners) for k in range(outer)]

    barrier = pltpu.get_barrier_semaphore()
    partners = [(near[r], ring[dy]) for dy in range(columns) for r in range(3) if (r, dy) != (1, 0)]
    partners += [(mates[k], column) for k in range(1, inner)]
    partners += [(across[k], column) for k in range(1, outer)]
    for partner in partners:
        pl.semaphore_signal(barrier, inc=1, device_id=partner, device_id_type=MESH)

    fetches = []
    for r in range(3):
        rows = pl.ds(pl.multiple_of(near[r] * columns, columns), columns)
        fetches.append(pltpu.make_async_copy(sub_ref.at[rows], lists.at[r], list_sem.at[r]))
        fetches.append(pltpu.make_async_copy(dest_ref.at[rows], dests.at[r], list_sem.at[3 + r]))
    for fetch in fetches:
        fetch.start()
    for fetch in fetches:
        fetch.wait()

    shape = (blocks, blocks)
    spot = lax.broadcasted_iota(jnp.int32, shape, 0) * blocks + lax.broadcasted_iota(jnp.int32, shape, 1)
    hops = [0] + [s for d in range(1, columns // 2 + 1) for s in dict.fromkeys((d, columns - d))]
    for dy in hops:
        for r in range(3):
            asked = lists[r, ring[dy]]
            mine = lax.shift_right_arithmetic(asked, tile_bits) == myself
            code = spot * tiles_per + (asked & (tiles_per - 1))
            first = jnp.min(jnp.where(mine, code, FAR)) & (tiles_per - 1)
            last = jnp.max(jnp.where(mine, code, -1)) & (tiles_per - 1)
            if (r, dy) == (1, 0):
                slot = (columns + column) * ROOM
                arrived[slot] = tiles_ref[first]
                arrived[slot + 1] = tiles_ref[last]
            else:
                packet[r * columns + dy, 0] = tiles_ref[first]
                packet[r * columns + dy, 1] = tiles_ref[last]

    pl.semaphore_wait(barrier, len(partners))
    sends = []
    for dy in hops:
        for r in range(3):
            if (r, dy) == (1, 0):
                continue
            sends.append(
                pltpu.make_async_remote_copy(
                    src_ref=packet.at[r * columns + dy],
                    dst_ref=arrived.at[pl.ds(((2 - r) * columns + column) * ROOM, ROOM)],
                    send_sem=send_sem.at[r * columns + dy],
                    recv_sem=recv_sem.at[r * columns + dy],
                    device_id=(near[r], ring[dy]),
                    device_id_type=MESH,
                )
            )
            sends[-1].start()

    nothing = 3 * columns * ROOM
    arrived[nothing] = jnp.zeros((edge, edge), BF16)
    own = lists[1, column]
    source = lax.shift_right_arithmetic(own, tile_bits)
    offset = lax.shift_right_arithmetic(source, column_bits) - owner + (owners + 1)
    offset = jnp.where(offset >= owners, offset - owners, offset)
    offset = jnp.where(offset >= owners, offset - owners, offset)
    base = (offset * columns + (source & (columns - 1))) * ROOM
    for p in range(blocks * blocks):
        here = spot == p
        entry = jnp.sum(jnp.where(here, own, 0))
        start = jnp.sum(jnp.where(here, base, 0))
        same = source == lax.shift_right_arithmetic(entry, tile_bits)
        rank = (jnp.min(jnp.where(same, spot, FAR)) < p).astype(jnp.int32)
        place[p] = jnp.where(entry >= 0, jnp.clip(start + rank, 0, nothing), nothing)

    row = lax.broadcasted_iota(jnp.int32, (columns, blocks), 0)
    lane = lax.broadcasted_iota(jnp.int32, (columns, blocks), 1)
    targets = [
        [jnp.sum(jnp.where((row == column) & (lane == i), dests[r], 0)) for i in range(blocks)]
        for r in range(3)
    ]
    chosen = [[jnp.int32(blocks) for _ in range(BACK)] for _ in range(3)]
    stored = [[jnp.int32(-1) for _ in range(BACK)] for _ in range(3)]
    for r in range(3):
        taken = jnp.int32(0)
        sent = jnp.int32(0)
        for i in range(blocks):
            target = targets[r][i]
            home = lax.shift_right_arithmetic(target, tile_bits + column_bits)
            mine = (target >= 0) & (home == owner)
            for k in range(BACK):
                stored[r][k] = jnp.where(mine & (taken == k), target & (tiles_per - 1), stored[r][k])
            taken = taken + mine.astype(jnp.int32)
            target = targets[1][i]
            home = lax.shift_right_arithmetic(target, tile_bits + column_bits)
            theirs = (target >= 0) & (home == near[r])
            for k in range(BACK):
                chosen[r][k] = jnp.where(theirs & (sent == k), i, chosen[r][k])
            sent = sent + theirs.astype(jnp.int32)

    for send in sends:
        send.wait()

    for i in range(blocks):
        for j in range(blocks):
            matrix[pl.ds(i * edge, edge), pl.ds(j * edge, edge)] = arrived[place[i * blocks + j]]

    chem = chem_ref[0]
    inverse = 1.0 / scale_ref[0]
    order = blocks * edge
    wide = 2 * edge

    def apply(u):
        high = u.astype(BF16)
        low = (u - high.astype(F32)).astype(BF16)
        both = jnp.concatenate([high, low], axis=0)
        parts = []
        for start in range(0, order, wide):
            cut = pl.ds(start, wide)
            w = dot(both, matrix[:, cut], ((1,), (0,))) + dot(both, matrix[cut, :], ((1,), (1,)))
            parts.append(0.5 * (w[:edge] + w[edge:]) - chem * u[:, start : start + wide])
        return jnp.concatenate(parts, axis=1) * inverse

    diagonal = lax.broadcasted_iota(jnp.int32, (edge, edge), 0) == lax.broadcasted_iota(
        jnp.int32, (edge, edge), 1
    )
    parts = []
    for j in range(blocks):
        upper = matrix[pl.ds(0, edge), pl.ds(j * edge, edge)].astype(F32)
        lower = matrix[pl.ds(j * edge, edge), pl.ds(0, edge)].astype(F32)
        part = 0.5 * (upper + lower.T)
        if j == 0:
            part = part - jnp.where(diagonal, chem, 0.0)
        parts.append(part * inverse)
    start = jnp.concatenate(parts, axis=1)
    first = 1.5 * start - 0.5 * apply(apply(start))
    once = apply(first)
    square = 1.5 * once - 0.5 * apply(apply(once))
    trace = 1.5 * jnp.sum(jnp.where(diagonal, first[:, :edge], 0.0)) - 0.5 * jnp.sum(first * square)
    trace = 0.5 * (edge - trace)

    groups = (
        (columns, column, [(owner, ring[k]) for k in range(columns)]),
        (inner, in_block, [(mates[k], column) for k in range(inner)]),
        (outer, lax.div(owner, inner), [(across[k], column) for k in range(outer)]),
    )

    def give(stage, value):
        count, at, group = groups[stage]
        trace_out[stage] = value
        trace_in[stage, at] = value
        copies = []
        for k in range(1, count):
            copies.append(
                pltpu.make_async_remote_copy(
                    src_ref=trace_out.at[stage],
                    dst_ref=trace_in.at[stage, at],
                    send_sem=trace_send.at[stage, k],
                    recv_sem=trace_recv.at[stage, k],
                    device_id=group[k],
                    device_id_type=MESH,
                )
            )
            copies[-1].start()
        return copies

    def take(stage, copies):
        for copy in copies:
            copy.wait()
        total = trace_in[stage, 0]
        for k in range(1, groups[stage][0]):
            total = total + trace_in[stage, k]
        return total

    copies = give(0, jnp.full((8, 128), trace, F32))
    once = apply(square)
    cube = 1.5 * once - 0.5 * apply(apply(once))
    last = 1.5 * first - 0.5 * cube
    for i in range(blocks):
        part = last[:, i * edge : (i + 1) * edge].T
        results[i] = 0.5 * (jnp.where(diagonal, 1.0, 0.0) - part) if i == 0 else -0.5 * part
    results[blocks] = jnp.zeros((edge, edge), F32)
    returns = []
    for r in (0, 2, 1):
        for k in range(BACK):
            if r == 1:
                back[1, k] = results[chosen[r][k]]
            else:
                going[r // 2, k] = results[chosen[r][k]]
        if r != 1:
            returns.append(
                pltpu.make_async_remote_copy(
                    src_ref=going.at[r // 2],
                    dst_ref=back.at[2 - r],
                    send_sem=back_send.at[r // 2],
                    recv_sem=back_recv.at[r // 2],
                    device_id=(near[r], column),
                    device_id_type=MESH,
                )
            )
            returns[-1].start()
    copies = give(1, take(0, copies))
    copies = give(2, take(1, copies))
    for copy in returns:
        copy.wait()
    weights = [
        [jnp.where(stored[r][k] == t, 1.0, 0.0).astype(F32) for r in range(3) for k in range(BACK)]
        for t in range(tiles_per)
    ]
    for at in range(0, edge, 8):
        pieces = [back[r, k, pl.ds(at, 8)] for r in range(3) for k in range(BACK)]
        for t in range(tiles_per):
            total = weights[t][0] * pieces[0]
            for weight, piece in zip(weights[t][1:], pieces[1:]):
                total = total + weight * piece
            out_ref[t, pl.ds(at, 8)] = total
    elec_ref[0] = 2.0 * jnp.max(take(2, copies))


def on_device(ks_tiles, chem_shift, spectral_scale, sub_tiles, result_dest):
    owners = lax.axis_size("owner")
    columns = lax.axis_size("col")
    tiles_per, edge = ks_tiles.shape[0], ks_tiles.shape[1]
    blocks = sub_tiles.shape[1]
    order = blocks * edge
    inner = min(8, owners)
    outer = owners // inner
    widest = max(columns, inner, outer)
    vmem, smem, hbm = pltpu.VMEM, pltpu.SMEM, pl.ANY
    dma = pltpu.SemaphoreType.DMA
    return pl.pallas_call(
        functools.partial(kernel, owners, columns, inner, blocks),
        out_shape=(
            jax.ShapeDtypeStruct((tiles_per, edge, edge), F32),
            jax.ShapeDtypeStruct((1,), F32),
        ),
        in_specs=[pl.BlockSpec(memory_space=s) for s in (smem, smem, vmem, hbm, hbm)],
        out_specs=[pl.BlockSpec(memory_space=s) for s in (vmem, smem)],
        scratch_shapes=[
            vmem((3, columns, blocks, blocks), jnp.int32),
            vmem((3, columns, blocks), jnp.int32),
            vmem((3 * columns, ROOM, edge, edge), BF16),
            vmem((3 * columns * ROOM + 1, edge, edge), BF16),
            smem((blocks * blocks,), jnp.int32),
            vmem((order, order), BF16),
            vmem((blocks + 1, edge, edge), F32),
            vmem((2, BACK, edge, edge), F32),
            vmem((3, BACK, edge, edge), F32),
            vmem((3, 8, 128), F32),
            vmem((3, widest, 8, 128), F32),
            dma((6,)),
            dma((3 * columns,)),
            dma((3 * columns,)),
            dma((2,)),
            dma((2,)),
            dma((3, widest)),
            dma((3, widest)),
        ],
        compiler_params=pltpu.CompilerParams(
            collective_id=0, has_side_effects=True, vmem_limit_bytes=48 * 2**20
        ),
        name="submatrix_density",
    )(chem_shift, spectral_scale, ks_tiles, sub_tiles, result_dest)


def solution(mesh):
    return jax.shard_map(
        on_device,
        mesh=mesh,
        in_specs=(P(("owner", "col"), None, None), P(), P(), P(), P()),
        out_specs=(P(("owner", "col"), None, None), P()),
        check_vma=False,
    )
```

time: 222 us -> 79 us (0.36)
  blocking collectives: 104 us -> 0 us
  Pallas kernels: 0 us -> 71.4 us
  waiting for transfers between devices: 35.1 us -> 0 us
  matrix products: 28.9 us -> 0 us
  starting transfers between devices: 27.7 us -> 0 us
  local copies, waits for them, and re-layouts: 14.7 us -> 3.5 us
  other arithmetic: 7.08 us -> 0 us
    psum x1 -> x0, blocking collectives: 104 us -> none  [on_device(): lax.psum(jnp.trace(density[:edge_len, :edge_len]), ('owner', 'col'))]
    pallas_call x0 -> x1, Pallas kernels: none -> 71.4 us  [on_device(): pl.pallas_call(functools.partial(kernel, owners, columns, inner, blocks),...]
    all_to_all x1 -> x0, waiting for transfers between devices: 31.7 us -> none  [on_device(): lax.all_to_all(sectioned, 'col', split_axis=1, concat_axis=1, tiled=True)]
    dot_general x6 -> x0, matrix products: 28.9 us -> none  [the longest x2 14.8 us: sign_density(): jnp.dot(current, current, precision=lax.Precision.HIGHEST, preferred_elem...]
    ppermute x4 -> x0, starting transfers between devices: 20.9 us -> none  [the longest x2 12.8 us: with_halo(): lax.ppermute(lax.slice_in_dim(block, block.shape[dim] - width, None, axis...]
    all_to_all x1 -> x0, starting transfers between devices: 6.82 us -> none  [on_device(): lax.all_to_all(sectioned, 'col', split_axis=1, concat_axis=1, tiled=True)]
    gather x5 -> x0, local copies, waits for them, and re-layouts: 5.12 us -> none  [the longest x1 2.18 us: on_device(): picked = jnp.take(arrived.reshape(-1, edge_len, edge_len), position, axis=0)]
    reduce_sum x6 -> x0, other arithmetic: 3.43 us -> none  [the longest x2 2.22 us: source_ranks(): return (device, jnp.sum(shared.astype(jnp.int32), axis=-1))]
  transfers between devices with their start and end apart: 5 -> 0, of which waited for: 2 -> 0; matrix products, arithmetic and copies ran while one was open for 2% -> 0% of each run, Pallas kernels for 0% -> 0%
where the time goes in v1:
time: 79 us; the launch traced here: 78.7 us
  Pallas kernels  71.4 us (90%)
  between operations  3.78 us (5%)
  local copies, waits for them, and re-layouts  3.5 us (4%)
    pallas_call x1, Pallas kernels, on_device(): pl.pallas_call(functools.partial(kernel, owners, columns, inner, blocks),...  71.4 us
    unnamed x5, local copies, waits for them, and re-layouts  3.5 us

profile of v1, /device:TPU:1, one launch (start us, length us, event | category | flops | bytes accessed | tf_op | source)
XLA Modules:
  0.0 78.7 jit_solution(4540556944020935028)
XLA Ops:
  0.6 0.0 copy-start
  2.0 0.9 %copy.8.dest_ref = s32[512,6]{1,0:T(8,128)S(1)} copy(s32[512,6]{0,1:T(8,128)} %param.9) | data formatting | bytes 24576 | tf_op args[4]
  2.9 1.7 %copy.7.sub_ref = s32[512,6,6]{2,1,0:T(8,128)S(1)} copy(s32[512,6,6]{0,2,1:T(8,128)} %param.8) | data formatting | bytes 147456 | tf_op args[3]
  4.5 0.0 copy-done
  4.5 71.4 %submatrix_density.1 = (f32[16,128,128]{2,1,0:T(8,128)S(1)}, f32[1]{0:T(128)}) custom-call(f32[1]{0:T(128)S(6)} %copy.11.chem_ref, f32[1]{0:T(128)S(6)} %copy.12.scale_ref, bf16[16,128,128]{2,1,0:T(8,128)(2,1)S(1)} %copy-done, s32[512,6,6]{2,1,0:T(8,128)S(1)} %copy.7.sub_ref, s32[512,6]{1,0:T(8,128)S(1)} %copy.8.dest_ref), custom_call_target="tpu_custom_call" | custom-call | tf_op jit(solution)/shard_map/submatrix_density/pallas_call | solution.py:268
  76.0 1.0 %copy.13 = f32[16,128,128]{2,1,0:T(8,128)} copy(f32[16,128,128]{2,1,0:T(8,128)S(1)} %get-tuple-element.4) | data formatting | bytes 2097152
Async XLA Ops:
  0.6 3.9 %copy-start = (bf16[16,128,128]{2,1,0:T(8,128)(2,1)S(1)}, bf16[16,128,128]{2,1,0:T(8,128)(2,1)}, u32[]{:S(2)}) copy-start(bf16[16,128,128]{2,1,0:T(8,128)(2,1)} %tiles_ref.1) | copy-start | bytes 1572868

commit v2 on v1

v2 whole, which is shorter than its diff:
```python
import functools
import jax
import jax.numpy as jnp
from jax import lax
from jax.experimental import pallas as pl
from jax.experimental.pallas import tpu as pltpu
from jax.sharding import PartitionSpec as P

F32 = jnp.float32
BF16 = jnp.bfloat16
MESH = pl.DeviceIdType.MESH
ROOM = 2
BACK = 3
FAR = 1 << 20


def log2(n):
    assert n & (n - 1) == 0
    return n.bit_length() - 1


def dot(a, b):
    return jnp.dot(a, b, preferred_element_type=F32)


def kernel(
    owners, columns, inner, blocks, chem_ref, scale_ref, tiles_hbm, sub_hbm, dest_hbm,
    out_ref, elec_ref, tiles_ref, lists, dests, packet, passing, arrived, place, high, low,
    results, going, back, trace_out, trace_in, fetch_sem, pass_sem, send_sem, recv_sem, back_send, back_recv,
    trace_send, trace_recv,
):
    tiles_per, edge = tiles_ref.shape[0], tiles_ref.shape[1]
    devices = owners * columns
    outer = owners // inner
    owner = lax.axis_index("owner")
    column = lax.axis_index("col")
    myself = owner * columns + column
    tile_bits, column_bits = log2(tiles_per), log2(columns)
    near = [lax.rem(owner + owners + r - 1, owners) for r in range(3)]
    ring = [lax.rem(column + dy, columns) for dy in range(columns)]
    in_block = lax.rem(owner, inner)
    block_start = owner - in_block
    mates = [block_start + lax.rem(in_block + k, inner) for k in range(inner)]
    across = [lax.rem(owner + k * inner, owners) for k in range(outer)]

    fetches = [
        pltpu.make_async_copy(there, here, fetch_sem.at[n])
        for n, (there, here) in enumerate(
            (
                (sub_hbm, lists),
                (tiles_hbm, tiles_ref),
                (dest_hbm, dests),
            )
        )
    ]
    for fetch in fetches:
        fetch.start()
    barrier = pltpu.get_barrier_semaphore()
    partners = [(near[r], ring[dy]) for dy in range(columns) for r in range(3) if (r, dy) != (1, 0)]
    partners += [(mates[k], column) for k in range(1, inner)]
    partners += [(across[k], column) for k in range(1, outer)]
    for partner in partners:
        pl.semaphore_signal(barrier, inc=1, device_id=partner, device_id_type=MESH)
    pl.semaphore_wait(barrier, len(partners))

    half = columns // 2
    turn = 1 - 2 * (owner & 1)
    at = [lax.rem(column + turn * k + columns, columns) for k in range(columns)]
    before = at[columns - 1]
    step = pltpu.make_async_remote_copy(
        src_ref=tiles_hbm,
        dst_ref=passing,
        send_sem=pass_sem.at[0],
        recv_sem=pass_sem.at[1],
        device_id=(owner, at[1]),
        device_id_type=MESH,
    )
    step.start()
    for fetch in fetches:
        fetch.wait()

    shape = (blocks, devices)
    lane = lax.broadcasted_iota(jnp.int32, shape, 1)
    row = lax.broadcasted_iota(jnp.int32, shape, 0)

    def asked_of(source):
        least, most = jnp.full(shape, FAR, jnp.int32), jnp.full(shape, -1, jnp.int32)
        for i in range(blocks):
            asked = lists[i]
            mine = lax.shift_right_arithmetic(asked, tile_bits) == source
            code = (row + i * blocks) * tiles_per + (asked & (tiles_per - 1))
            least = jnp.minimum(least, jnp.where(mine, code, FAR))
            most = jnp.maximum(most, jnp.where(mine, code, -1))
        least = jnp.min(least, axis=0, keepdims=True) & (tiles_per - 1)
        most = jnp.max(most, axis=0, keepdims=True) & (tiles_per - 1)
        return least * tiles_per + most

    sends = []

    def pack(asked, tiles, r, to, ref, slot):
        both = jnp.sum(jnp.where(lane[:1] == near[r] * columns + to, asked, 0))
        ref[slot] = tiles[lax.shift_right_arithmetic(both, tile_bits)]
        ref[slot + 1] = tiles[both & (tiles_per - 1)]

    def send(asked, tiles, r, k, source, to):
        slot = (r * columns + k) * ROOM
        pack(asked, tiles, r, to, packet, slot)
        sends.append(
            pltpu.make_async_remote_copy(
                src_ref=packet.at[pl.ds(slot, ROOM)],
                dst_ref=arrived.at[pl.ds(((2 - r) * columns + source) * ROOM, ROOM)],
                send_sem=send_sem.at[r * columns + k],
                recv_sem=recv_sem.at[r * columns + k],
                device_id=(near[r], to),
                device_id_type=MESH,
            )
        )
        sends[-1].start()

    asked = asked_of(myself)
    for k in [*range(columns - 1, half, -1), 0]:
        for r in range(3):
            if (r, k) != (1, 0):
                send(asked, tiles_ref, r, k, column, at[k])
    pack(asked, tiles_ref, 1, column, arrived, (columns + column) * ROOM)
    asked = asked_of(owner * columns + before)

    nothing = 3 * columns * ROOM
    arrived[nothing] = jnp.zeros((edge, edge), BF16)
    across_i = lax.broadcasted_iota(jnp.int32, (blocks, blocks), 1)
    spot = across_i * blocks + lax.broadcasted_iota(jnp.int32, (blocks, blocks), 0)
    own = jnp.zeros((blocks, blocks), jnp.int32)
    for i in range(blocks):
        held = jnp.sum(jnp.where(lane == myself, lists[i], 0), axis=1, keepdims=True)
        own = own + jnp.where(across_i == i, held, 0)
    source = lax.shift_right_arithmetic(own, tile_bits)
    offset = lax.shift_right_arithmetic(source, column_bits) - owner + (owners + 1)
    offset = jnp.where(offset >= owners, offset - owners, offset)
    offset = jnp.where(offset >= owners, offset - owners, offset)
    base = (offset * columns + (source & (columns - 1))) * ROOM
    for p in range(blocks * blocks):
        here = spot == p
        entry = jnp.sum(jnp.where(here, own, 0))
        start = jnp.sum(jnp.where(here, base, 0))
        same = source == lax.shift_right_arithmetic(entry, tile_bits)
        rank = (jnp.min(jnp.where(same, spot, FAR)) < p).astype(jnp.int32)
        place[p] = jnp.where(entry >= 0, jnp.clip(start + rank, 0, nothing), nothing)

    step.wait()
    for k in range(half, 0, -1):
        for r in range(3):
            if (r, k) != (1, 1):
                send(asked, passing, r, k, before, at[k - 1])
    pack(asked, passing, 1, column, arrived, (columns + before) * ROOM)

    targets = [
        [
            jnp.sum(jnp.where((lane == near[r] * columns + column) & (row == i), dests[...], 0))
            for i in range(blocks)
        ]
        for r in range(3)
    ]
    chosen = [[jnp.int32(blocks) for _ in range(BACK)] for _ in range(3)]
    stored = [[jnp.int32(-1) for _ in range(BACK)] for _ in range(3)]
    for r in range(3):
        taken = jnp.int32(0)
        sent = jnp.int32(0)
        for i in range(blocks):
            target = targets[r][i]
            home = lax.shift_right_arithmetic(target, tile_bits + column_bits)
            mine = (target >= 0) & (home == owner)
            for k in range(BACK):
                stored[r][k] = jnp.where(mine & (taken == k), target & (tiles_per - 1), stored[r][k])
            taken = taken + mine.astype(jnp.int32)
            target = targets[1][i]
            home = lax.shift_right_arithmetic(target, tile_bits + column_bits)
            theirs = (target >= 0) & (home == near[r])
            for k in range(BACK):
                chosen[r][k] = jnp.where(theirs & (sent == k), i, chosen[r][k])
            sent = sent + theirs.astype(jnp.int32)

    for copy in sends:
        copy.wait()

    chem = chem_ref[...]
    inverse = 1.0 / scale_ref[...]
    order = blocks * edge
    wide = 2 * edge
    diagonal = lax.broadcasted_iota(jnp.int32, (edge, edge), 0) == lax.broadcasted_iota(
        jnp.int32, (edge, edge), 1
    )
    parts = []
    for i in range(blocks):
        for j in range(blocks):
            part = arrived[place[i * blocks + j]].astype(F32)
            part = part + arrived[place[j * blocks + i]].T.astype(F32)
            part = part * (0.5 * inverse)
            if i == j:
                part = part - jnp.where(diagonal, chem * inverse, 0.0)
            rows, cols = pl.ds(i * edge, edge), pl.ds(j * edge, edge)
            upper = part.astype(BF16)
            high[rows, cols] = upper
            low[rows, cols] = (part - upper.astype(F32)).astype(BF16)
            if i == 0:
                parts.append(part)
    start = jnp.concatenate(parts, axis=1)

    def apply(u):
        upper = u.astype(BF16)
        lower = (u - upper.astype(F32)).astype(BF16)
        both = jnp.concatenate([upper, lower], axis=0)
        parts = []
        for at in range(0, order, wide):
            cut = pl.ds(at, wide)
            w = dot(both, high[:, cut])
            parts.append(w[:edge] + w[edge:] + dot(upper, low[:, cut]))
        return jnp.concatenate(parts, axis=1)

    first = 1.5 * start - 0.5 * apply(apply(start))
    once = apply(first)
    twice = apply(once)
    cubed = 1.5 * jnp.sum(first * once) - 0.5 * jnp.sum(once * twice)
    trace = 1.5 * jnp.sum(jnp.where(diagonal, first[:, :edge], 0.0)) - 0.5 * cubed
    trace = 0.5 * (edge - trace)

    groups = (
        (columns, column, [(owner, ring[k]) for k in range(columns)]),
        (inner, in_block, [(mates[k], column) for k in range(inner)]),
        (outer, lax.div(owner, inner), [(across[k], column) for k in range(outer)]),
    )

    def give(stage, value):
        count, at, group = groups[stage]
        trace_out[stage] = value
        trace_in[stage, at] = value
        copies = []
        for k in range(1, count):
            copies.append(
                pltpu.make_async_remote_copy(
                    src_ref=trace_out.at[stage],
                    dst_ref=trace_in.at[stage, at],
                    send_sem=trace_send.at[stage, k],
                    recv_sem=trace_recv.at[stage, k],
                    device_id=group[k],
                    device_id_type=MESH,
                )
            )
            copies[-1].start()
        return copies

    def take(stage, copies):
        for copy in copies:
            copy.wait()
        total = trace_in[stage, 0]
        for k in range(1, groups[stage][0]):
            total = total + trace_in[stage, k]
        return total

    copies = give(0, jnp.full((8, 128), trace, F32))
    square = 1.5 * once - 0.5 * apply(twice)
    once = apply(square)
    copies = give(1, take(0, copies))
    twice = apply(once)
    cube = 1.5 * once - 0.5 * apply(twice)
    last = 1.5 * first - 0.5 * cube
    copies = give(2, take(1, copies))
    for i in range(blocks):
        part = last[:, i * edge : (i + 1) * edge].T
        results[i] = 0.5 * (jnp.where(diagonal, 1.0, 0.0) - part) if i == 0 else -0.5 * part
    results[blocks] = jnp.zeros((edge, edge), F32)
    returns = []
    for r in (0, 2, 1):
        for k in range(BACK):
            if r == 1:
                back[1, k] = results[chosen[r][k]]
            else:
                going[r // 2, k] = results[chosen[r][k]]
        if r != 1:
            returns.append(
                pltpu.make_async_remote_copy(
                    src_ref=going.at[r // 2],
                    dst_ref=back.at[2 - r],
                    send_sem=back_send.at[r // 2],
                    recv_sem=back_recv.at[r // 2],
                    device_id=(near[r], column),
                    device_id_type=MESH,
                )
            )
            returns[-1].start()
    for copy in returns:
        copy.wait()
    weights = [
        [jnp.where(stored[r][k] == t, 1.0, 0.0).astype(F32) for r in range(3) for k in range(BACK)]
        for t in range(tiles_per)
    ]
    for at in range(0, edge, 8):
        pieces = [back[r, k, pl.ds(at, 8)] for r in range(3) for k in range(BACK)]
        for t in range(tiles_per):
            total = weights[t][0] * pieces[0]
            for weight, piece in zip(weights[t][1:], pieces[1:]):
                total = total + weight * piece
            out_ref[t, pl.ds(at, 8)] = total
    elec_ref[...] = 2.0 * take(2, copies)[:1]


def on_device(ks_tiles, chem_shift, spectral_scale, sub_tiles, result_dest):
    owners = lax.axis_size("owner")
    columns = lax.axis_size("col")
    tiles_per, edge = ks_tiles.shape[0], ks_tiles.shape[1]
    blocks = sub_tiles.shape[1]
    order = blocks * edge
    inner = min(8, owners)
    outer = owners // inner
    widest = max(columns, inner, outer)
    vmem, smem, hbm = pltpu.VMEM, pltpu.SMEM, pl.ANY
    dma = pltpu.SemaphoreType.DMA
    density, electrons = pl.pallas_call(
        functools.partial(kernel, owners, columns, inner, blocks),
        out_shape=(
            jax.ShapeDtypeStruct((tiles_per, edge, edge), F32),
            jax.ShapeDtypeStruct((1, 128), F32),
        ),
        in_specs=[pl.BlockSpec(memory_space=vmem)] * 2 + [pl.BlockSpec(memory_space=hbm)] * 3,
        out_specs=[pl.BlockSpec(memory_space=vmem)] * 2,
        scratch_shapes=[
            vmem((tiles_per, edge, edge), BF16),
            vmem((blocks, blocks, owners * columns), jnp.int32),
            vmem((blocks, owners * columns), jnp.int32),
            vmem((3 * columns * ROOM, edge, edge), BF16),
            vmem((tiles_per, edge, edge), BF16),
            vmem((3 * columns * ROOM + 1, edge, edge), BF16),
            smem((blocks * blocks,), jnp.int32),
            vmem((order, order), BF16),
            vmem((order, order), BF16),
            vmem((blocks + 1, edge, edge), F32),
            vmem((2, BACK, edge, edge), F32),
            vmem((3, BACK, edge, edge), F32),
            vmem((3, 8, 128), F32),
            vmem((3, widest, 8, 128), F32),
            dma((3,)),
            dma((2,)),
            dma((3 * columns,)),
            dma((3 * columns,)),
            dma((2,)),
            dma((2,)),
            dma((3, widest)),
            dma((3, widest)),
        ],
        compiler_params=pltpu.CompilerParams(
            collective_id=0, has_side_effects=True, vmem_limit_bytes=48 * 2**20
        ),
        name="submatrix_density",
    )(
        chem_shift.reshape(1, 1),
        spectral_scale.reshape(1, 1),
        *(
            pltpu.with_memory_space_constraint(a, pltpu.HBM)
            for a in (
                ks_tiles,
                jnp.transpose(sub_tiles, (1, 2, 0)),
                result_dest.T,
            )
        )
    )
    return density, electrons[0, :1]


def solution(mesh):
    return jax.shard_map(
        on_device,
        mesh=mesh,
        in_specs=(P(("owner", "col"), None, None), P(), P(), P(), P()),
        out_specs=(P(("owner", "col"), None, None), P()),
        check_vma=False,
    )
```

time: 79 us -> 73.2 us (0.927)
  the two profiles are of different devices: /device:TPU:1 before, /device:TPU:8 now
where the time goes in v2:
time: 73.2 us; the launch traced here: 73.1 us
  Pallas kernels  69 us (94%)
  between operations  3.09 us (4%)
  local copies, waits for them, and re-layouts  0.97 us (1%)
    pallas_call x1, Pallas kernels, on_device(): pl.pallas_call(functools.partial(kernel, owners, columns, inner, blocks),...  69 us

profile of v2, /device:TPU:8, one launch (start us, length us, event | category | flops | bytes accessed | tf_op | source)
XLA Modules:
  0.0 73.1 jit_solution(2541855212711406235)
XLA Ops:
  1.9 69.0 %submatrix_density.1 = (f32[16,128,128]{2,1,0:T(8,128)S(1)}, f32[1,128]{1,0:T(1,128)S(1)}) custom-call(f32[1,1]{1,0:T(1,128)} %bitcast.6.chem_ref, f32[1,1]{1,0:T(1,128)} %bitcast.7.scale_ref, bf16[16,128,128]{2,1,0:T(8,128)(2,1)} %tiles_hbm.1, s32[6,6,512]{2,1,0:T(8,128)} %bitcast.9, s32[6,512]{1,0:T(8,128)} %bitcast.10), custom_call_target="tpu_custom_call" | custom-call | tf_op jit(solution)/shard_map/submatrix_density/pallas_call | solution.py:317
  70.9 1.0 %copy.11 = f32[16,128,128]{2,1,0:T(8,128)} copy(f32[16,128,128]{2,1,0:T(8,128)S(1)} %get-tuple-element.8) | data formatting | bytes 2097152

commit v3 on v2

--- a/solution.py
+++ b/solution.py
@@ -1,4 +1,5 @@
 import functools
+import itertools
 import jax
 import jax.numpy as jnp
 from jax import lax
@@ -24,24 +25,23 @@
 
 
 def kernel(
-    owners, columns, inner, blocks, chem_ref, scale_ref, tiles_hbm, sub_hbm, dest_hbm,
+    owners, columns, blocks, chem_ref, scale_ref, tiles_hbm, sub_hbm, dest_hbm,
     out_ref, elec_ref, tiles_ref, lists, dests, packet, passing, arrived, place, high, low,
     results, going, back, trace_out, trace_in, fetch_sem, pass_sem, send_sem, recv_sem, back_send, back_recv,
-    trace_send, trace_recv,
+    trace_send, trace_recv, ready,
 ):
     tiles_per, edge = tiles_ref.shape[0], tiles_ref.shape[1]
     devices = owners * columns
-    outer = owners // inner
     owner = lax.axis_index("owner")
     column = lax.axis_index("col")
     myself = owner * columns + column
     tile_bits, column_bits = log2(tiles_per), log2(columns)
     near = [lax.rem(owner + owners + r - 1, owners) for r in range(3)]
-    ring = [lax.rem(column + dy, columns) for dy in range(columns)]
-    in_block = lax.rem(owner, inner)
-    block_start = owner - in_block
-    mates = [block_start + lax.rem(in_block + k, inner) for k in range(inner)]
-    across = [lax.rem(owner + k * inner, owners) for k in range(outer)]
+    half = columns // 2
+    core = owner & 1
+    turn = 1 - 2 * core
+    at = [lax.rem(column + turn * k + columns, columns) for k in range(columns)]
+    before = at[columns - 1]
 
     fetches = [
         pltpu.make_async_copy(there, here, fetch_sem.at[n])
@@ -55,18 +55,16 @@
     ]
     for fetch in fetches:
         fetch.start()
+    beside = [(owner, at[1]), (owner, before), (near[0], column), (near[2], column)]
     barrier = pltpu.get_barrier_semaphore()
-    partners = [(near[r], ring[dy]) for dy in range(columns) for r in range(3) if (r, dy) != (1, 0)]
-    partners += [(mates[k], column) for k in range(1, inner)]
-    partners += [(across[k], column) for k in range(1, outer)]
-    for partner in partners:
-        pl.semaphore_signal(barrier, inc=1, device_id=partner, device_id_type=MESH)
-    pl.semaphore_wait(barrier, len(partners))
-
-    half = columns // 2
-    turn = 1 - 2 * (owner & 1)
-    at = [lax.rem(column + turn * k + columns, columns) for k in range(columns)]
-    before = at[columns - 1]
+
+    def tell(sem, partners):
+        for partner in partners:
+            pl.semaphore_signal(sem, inc=1, device_id=partner, device_id_type=MESH)
+
+    tell(barrier, beside)
+    pl.semaphore_wait(barrier, len(beside))
+
     step = pltpu.make_async_remote_copy(
         src_ref=tiles_hbm,
         dst_ref=passing,
@@ -76,6 +74,7 @@
         device_id_type=MESH,
     )
     step.start()
+    tell(ready.at[0], beside)
     for fetch in fetches:
         fetch.wait()
 
@@ -118,10 +117,17 @@
         sends[-1].start()
 
     asked = asked_of(myself)
-    for k in [*range(columns - 1, half, -1), 0]:
+    pl.semaphore_wait(ready.at[0], len(beside))
+    over = [(owner, at[2]), (owner, at[columns - 2])]
+    tell(ready.at[1], over)
+    for k in (columns - 1, 0):
         for r in range(3):
             if (r, k) != (1, 0):
                 send(asked, tiles_ref, r, k, column, at[k])
+    pl.semaphore_wait(ready.at[1], len(over))
+    for k in range(columns - 2, half, -1):
+        for r in range(3):
+            send(asked, tiles_ref, r, k, column, at[k])
     pack(asked, tiles_ref, 1, column, arrived, (columns + column) * ROOM)
     asked = asked_of(owner * columns + before)
 
@@ -152,6 +158,16 @@
             if (r, k) != (1, 1):
                 send(asked, passing, r, k, before, at[k - 1])
     pack(asked, passing, 1, column, arrived, (columns + before) * ROOM)
+
+    reach, stage = 1, 2
+    while 2 * reach <= max(2, owners // 2):
+        far = [
+            (lax.rem(owner + reach, owners), column),
+            (lax.rem(owner + owners - reach, owners), column),
+        ]
+        tell(ready.at[stage], far)
+        pl.semaphore_wait(ready.at[stage], 2)
+        reach, stage = 2 * reach, stage + 1
 
     targets = [
         [
@@ -190,19 +206,18 @@
         jnp.int32, (edge, edge), 1
     )
     parts = []
-    for i in range(blocks):
-        for j in range(blocks):
-            part = arrived[place[i * blocks + j]].astype(F32)
-            part = part + arrived[place[j * blocks + i]].T.astype(F32)
-            part = part * (0.5 * inverse)
-            if i == j:
-                part = part - jnp.where(diagonal, chem * inverse, 0.0)
-            rows, cols = pl.ds(i * edge, edge), pl.ds(j * edge, edge)
-            upper = part.astype(BF16)
-            high[rows, cols] = upper
-            low[rows, cols] = (part - upper.astype(F32)).astype(BF16)
-            if i == 0:
-                parts.append(part)
+    for i, j in sorted(itertools.product(range(blocks), repeat=2), key=lambda p: (p[0] > 0, p[1])):
+        part = arrived[place[i * blocks + j]].astype(F32)
+        part = part + arrived[place[j * blocks + i]].T.astype(F32)
+        part = part * (0.5 * inverse)
+        if i == j:
+            part = part - jnp.where(diagonal, chem * inverse, 0.0)
+        rows, cols = pl.ds(i * edge, edge), pl.ds(j * edge, edge)
+        upper = part.astype(BF16)
+        high[rows, cols] = upper
+        low[rows, cols] = (part - upper.astype(F32)).astype(BF16)
+        if i == 0:
+            parts.append(part)
     start = jnp.concatenate(parts, axis=1)
 
     def apply(u):
@@ -223,25 +238,49 @@
     trace = 1.5 * jnp.sum(jnp.where(diagonal, first[:, :edge], 0.0)) - 0.5 * cubed
     trace = 0.5 * (edge - trace)
 
+    inner = min(8, owners)
+    width, depth = inner // 2, owners // inner
+    here_x, here_z = lax.div(lax.rem(owner, inner), 2), lax.div(owner, inner)
+
+    def steps(*sizes):
+        every = list(itertools.product(*(range(size) for size in sizes)))[1:]
+        return sorted(every, key=lambda p: -sum(min(n, size - n) for n, size in zip(p, sizes)))
+
     groups = (
-        (columns, column, [(owner, ring[k]) for k in range(columns)]),
-        (inner, in_block, [(mates[k], column) for k in range(inner)]),
-        (outer, lax.div(owner, inner), [(across[k], column) for k in range(outer)]),
+        (
+            2 * columns,
+            core * columns + column,
+            [
+                (owner - core + lax.rem(core + dc, 2), lax.rem(column + dy, columns))
+                for dy, dc in steps(columns, 2)
+            ],
+        ),
+        (
+            owners // 2,
+            lax.div(owner, 2),
+            [
+                (
+                    lax.rem(here_z + dz, depth) * inner + lax.rem(here_x + dx, width) * 2 + core,
+                    column,
+                )
+                for dz, dx in steps(depth, width)
+            ],
+        ),
     )
 
     def give(stage, value):
-        count, at, group = groups[stage]
+        place_in = groups[stage][1]
         trace_out[stage] = value
-        trace_in[stage, at] = value
+        trace_in[stage, place_in] = value
         copies = []
-        for k in range(1, count):
+        for k, partner in enumerate(groups[stage][2]):
             copies.append(
                 pltpu.make_async_remote_copy(
                     src_ref=trace_out.at[stage],
-                    dst_ref=trace_in.at[stage, at],
+                    dst_ref=trace_in.at[stage, place_in],
                     send_sem=trace_send.at[stage, k],
                     recv_sem=trace_recv.at[stage, k],
-                    device_id=group[k],
+                    device_id=partner,
                     device_id_type=MESH,
                 )
             )
@@ -250,20 +289,17 @@
 
     def take(stage, copies):
         for copy in copies:
-            copy.wait()
+            copy.wait_recv()
         total = trace_in[stage, 0]
         for k in range(1, groups[stage][0]):
             total = total + trace_in[stage, k]
         return total
 
-    copies = give(0, jnp.full((8, 128), trace, F32))
+    first_copies = give(0, jnp.full((1, 128), trace, F32))
     square = 1.5 * once - 0.5 * apply(twice)
     once = apply(square)
-    copies = give(1, take(0, copies))
-    twice = apply(once)
-    cube = 1.5 * once - 0.5 * apply(twice)
+    cube = 1.5 * once - 0.5 * apply(apply(once))
     last = 1.5 * first - 0.5 * cube
-    copies = give(2, take(1, copies))
     for i in range(blocks):
         part = last[:, i * edge : (i + 1) * edge].T
         results[i] = 0.5 * (jnp.where(diagonal, 1.0, 0.0) - part) if i == 0 else -0.5 * part
@@ -287,6 +323,7 @@
                 )
             )
             returns[-1].start()
+    last_copies = give(1, take(0, first_copies))
     for copy in returns:
         copy.wait()
     weights = [
@@ -300,7 +337,9 @@
             for weight, piece in zip(weights[t][1:], pieces[1:]):
                 total = total + weight * piece
             out_ref[t, pl.ds(at, 8)] = total
-    elec_ref[...] = 2.0 * take(2, copies)[:1]
+    elec_ref[...] = 2.0 * take(1, last_copies)
+    for copy in first_copies + last_copies:
+        copy.wait_send()
 
 
 def on_device(ks_tiles, chem_shift, spectral_scale, sub_tiles, result_dest):
@@ -309,13 +348,11 @@
     tiles_per, edge = ks_tiles.shape[0], ks_tiles.shape[1]
     blocks = sub_tiles.shape[1]
     order = blocks * edge
-    inner = min(8, owners)
-    outer = owners // inner
-    widest = max(columns, inner, outer)
+    widest = max(2 * columns, owners // 2)
     vmem, smem, hbm = pltpu.VMEM, pltpu.SMEM, pl.ANY
     dma = pltpu.SemaphoreType.DMA
     density, electrons = pl.pallas_call(
-        functools.partial(kernel, owners, columns, inner, blocks),
+        functools.partial(kernel, owners, columns, blocks),
         out_shape=(
             jax.ShapeDtypeStruct((tiles_per, edge, edge), F32),
             jax.ShapeDtypeStruct((1, 128), F32),
@@ -335,16 +372,17 @@
             vmem((blocks + 1, edge, edge), F32),
             vmem((2, BACK, edge, edge), F32),
             vmem((3, BACK, edge, edge), F32),
-            vmem((3, 8, 128), F32),
-            vmem((3, widest, 8, 128), F32),
+            vmem((2, 1, 128), F32),
+            vmem((2, widest, 1, 128), F32),
             dma((3,)),
             dma((2,)),
             dma((3 * columns,)),
             dma((3 * columns,)),
             dma((2,)),
             dma((2,)),
-            dma((3, widest)),
-            dma((3, widest)),
+            dma((2, widest)),
+            dma((2, widest)),
+            pltpu.SemaphoreType.REGULAR((2 + log2(owners),)),
         ],
         compiler_params=pltpu.CompilerParams(
             collective_id=0, has_side_effects=True, vmem_limit_bytes=48 * 2**20

time: 73.2 us -> 66.6 us (0.910)
  the two profiles are of different devices: /device:TPU:8 before, /device:TPU:1 now
where the time goes in v3:
time: 66.6 us; the launch traced here: 66.4 us
  Pallas kernels  62.4 us (94%)
  between operations  3.09 us (5%)
  local copies, waits for them, and re-layouts  0.97 us (1%)
    pallas_call x1, Pallas kernels, on_device(): pl.pallas_call(functools.partial(kernel, owners, columns, blocks), out_sh...  62.4 us

profile of v3, /device:TPU:1, one launch (start us, length us, event | category | flops | bytes accessed | tf_op | source)
XLA Modules:
  0.0 66.4 jit_solution(5885125773823825904)
XLA Ops:
  1.9 62.4 %submatrix_density.1 = (f32[16,128,128]{2,1,0:T(8,128)S(1)}, f32[1,128]{1,0:T(1,128)S(1)}) custom-call(f32[1,1]{1,0:T(1,128)} %bitcast.6.chem_ref, f32[1,1]{1,0:T(1,128)} %bitcast.7.scale_ref, bf16[16,128,128]{2,1,0:T(8,128)(2,1)} %tiles_hbm.1, s32[6,6,512]{2,1,0:T(8,128)} %bitcast.9, s32[6,512]{1,0:T(8,128)} %bitcast.10), custom_call_target="tpu_custom_call" | custom-call | tf_op jit(solution)/shard_map/submatrix_density/pallas_call | solution.py:354
  64.3 1.0 %copy.11 = f32[16,128,128]{2,1,0:T(8,128)} copy(f32[16,128,128]{2,1,0:T(8,128)S(1)} %get-tuple-element.8) | data formatting | bytes 2097152

commit v4 on v3

--- a/solution.py
+++ b/solution.py
@@ -247,23 +247,18 @@
         return sorted(every, key=lambda p: -sum(min(n, size - n) for n, size in zip(p, sizes)))
 
     groups = (
+        (columns, column, [(owner, lax.rem(column + dy, columns)) for (dy,) in steps(columns)]),
         (
-            2 * columns,
-            core * columns + column,
-            [
-                (owner - core + lax.rem(core + dc, 2), lax.rem(column + dy, columns))
-                for dy, dc in steps(columns, 2)
-            ],
-        ),
-        (
-            owners // 2,
-            lax.div(owner, 2),
+            owners,
+            owner,
             [
                 (
-                    lax.rem(here_z + dz, depth) * inner + lax.rem(here_x + dx, width) * 2 + core,
+                    lax.rem(here_z + dz, depth) * inner
+                    + lax.rem(here_x + dx, width) * 2
+                    + lax.rem(core + dc, 2),
                     column,
                 )
-                for dz, dx in steps(depth, width)
+                for dz, dx, dc in steps(depth, width, 2)
             ],
         ),
     )
@@ -337,9 +332,9 @@
             for weight, piece in zip(weights[t][1:], pieces[1:]):
                 total = total + weight * piece
             out_ref[t, pl.ds(at, 8)] = total
-    elec_ref[...] = 2.0 * take(1, last_copies)
     for copy in first_copies + last_copies:
         copy.wait_send()
+    elec_ref[...] = jnp.broadcast_to(2.0 * take(1, last_copies), elec_ref.shape)
 
 
 def on_device(ks_tiles, chem_shift, spectral_scale, sub_tiles, result_dest):
@@ -348,14 +343,14 @@
     tiles_per, edge = ks_tiles.shape[0], ks_tiles.shape[1]
     blocks = sub_tiles.shape[1]
     order = blocks * edge
-    widest = max(2 * columns, owners // 2)
+    widest = max(columns, owners)
     vmem, smem, hbm = pltpu.VMEM, pltpu.SMEM, pl.ANY
     dma = pltpu.SemaphoreType.DMA
     density, electrons = pl.pallas_call(
         functools.partial(kernel, owners, columns, blocks),
         out_shape=(
             jax.ShapeDtypeStruct((tiles_per, edge, edge), F32),
-            jax.ShapeDtypeStruct((1, 128), F32),
+            jax.ShapeDtypeStruct((8, 128), F32),
         ),
         in_specs=[pl.BlockSpec(memory_space=vmem)] * 2 + [pl.BlockSpec(memory_space=hbm)] * 3,
         out_specs=[pl.BlockSpec(memory_space=vmem)] * 2,

time: 66.6 us -> 67.9 us (1.020)
  Pallas kernels: 62.4 us -> 64.4 us
  between operations: 3.09 us -> 1.93 us
    pallas_call x1, Pallas kernels: 62.4 us -> 64.4 us  [on_device(): pl.pallas_call(functools.partial(kernel, owners, columns, blocks), out_sh...]
where the time goes in v4:
time: 67.9 us; the launch traced here: 67.8 us
  Pallas kernels  64.4 us (95%)
  between operations  1.93 us (3%)
  local copies, waits for them, and re-layouts  1.48 us (2%)
    pallas_call x1, Pallas kernels, on_device(): pl.pallas_call(functools.partial(kernel, owners, columns, blocks), out_sh...  64.4 us

profile of v4, /device:TPU:1, one launch (start us, length us, event | category | flops | bytes accessed | tf_op | source)
XLA Modules:
  0.0 67.8 jit_solution(10786597695427197399)
XLA Ops:
  1.9 64.4 %submatrix_density.1 = (f32[16,128,128]{2,1,0:T(8,128)S(1)}, f32[8,128]{1,0:T(8,128)S(1)}) custom-call(f32[1,1]{1,0:T(1,128)} %bitcast.5.chem_ref, f32[1,1]{1,0:T(1,128)} %bitcast.6.scale_ref, bf16[16,128,128]{2,1,0:T(8,128)(2,1)} %tiles_hbm.1, s32[6,6,512]{2,1,0:T(8,128)} %bitcast.7, s32[6,512]{1,0:T(8,128)} %bitcast.8), custom_call_target="tpu_custom_call" | custom-call | tf_op jit(solution)/shard_map/submatrix_density/pallas_call | solution.py:349
  66.3 0.5 slice.3
  66.8 1.0 %copy.10 = f32[16,128,128]{2,1,0:T(8,128)} copy(f32[16,128,128]{2,1,0:T(8,128)S(1)} %get-tuple-element.8) | data formatting | bytes 2097152

commit v5 on v3

--- a/solution.py
+++ b/solution.py
@@ -337,9 +337,9 @@
             for weight, piece in zip(weights[t][1:], pieces[1:]):
                 total = total + weight * piece
             out_ref[t, pl.ds(at, 8)] = total
-    elec_ref[...] = 2.0 * take(1, last_copies)
     for copy in first_copies + last_copies:
         copy.wait_send()
+    elec_ref[...] = jnp.broadcast_to(2.0 * take(1, last_copies), elec_ref.shape)
 
 
 def on_device(ks_tiles, chem_shift, spectral_scale, sub_tiles, result_dest):
@@ -355,7 +355,7 @@
         functools.partial(kernel, owners, columns, blocks),
         out_shape=(
             jax.ShapeDtypeStruct((tiles_per, edge, edge), F32),
-            jax.ShapeDtypeStruct((1, 128), F32),
+            jax.ShapeDtypeStruct((8, 128), F32),
         ),
         in_specs=[pl.BlockSpec(memory_space=vmem)] * 2 + [pl.BlockSpec(memory_space=hbm)] * 3,
         out_specs=[pl.BlockSpec(memory_space=vmem)] * 2,

time: 66.6 us -> 65.9 us (0.989)
  between operations: 3.09 us -> 1.93 us
where the time goes in v5:
time: 65.9 us; the launch traced here: 65.7 us
  Pallas kernels  62.3 us (95%)
  between operations  1.93 us (3%)
  local copies, waits for them, and re-layouts  1.48 us (2%)
    pallas_call x1, Pallas kernels, on_device(): pl.pallas_call(functools.partial(kernel, owners, columns, blocks), out_sh...  62.3 us

profile of v5, /device:TPU:1, one launch (start us, length us, event | category | flops | bytes accessed | tf_op | source)
XLA Modules:
  0.0 65.7 jit_solution(17262801526185969075)
XLA Ops:
  1.9 62.3 %submatrix_density.1 = (f32[16,128,128]{2,1,0:T(8,128)S(1)}, f32[8,128]{1,0:T(8,128)S(1)}) custom-call(f32[1,1]{1,0:T(1,128)} %bitcast.5.chem_ref, f32[1,1]{1,0:T(1,128)} %bitcast.6.scale_ref, bf16[16,128,128]{2,1,0:T(8,128)(2,1)} %tiles_hbm.1, s32[6,6,512]{2,1,0:T(8,128)} %bitcast.7, s32[6,512]{1,0:T(8,128)} %bitcast.8), custom_call_target="tpu_custom_call" | custom-call | tf_op jit(solution)/shard_map/submatrix_density/pallas_call | solution.py:354
  64.2 0.5 slice.3
  64.8 1.0 %copy.10 = f32[16,128,128]{2,1,0:T(8,128)} copy(f32[16,128,128]{2,1,0:T(8,128)S(1)} %get-tuple-element.8) | data formatting | bytes 2097152

commit v6 on v5

--- a/solution.py
+++ b/solution.py
@@ -36,12 +36,21 @@
     column = lax.axis_index("col")
     myself = owner * columns + column
     tile_bits, column_bits = log2(tiles_per), log2(columns)
-    near = [lax.rem(owner + owners + r - 1, owners) for r in range(3)]
+    near = [(owner + r - 1) & (owners - 1) for r in range(3)]
     half = columns // 2
     core = owner & 1
     turn = 1 - 2 * core
-    at = [lax.rem(column + turn * k + columns, columns) for k in range(columns)]
+    at = [(column + turn * k) & (columns - 1) for k in range(columns)]
     before = at[columns - 1]
+
+    beside = [(owner, at[1]), (owner, before), (near[0], column), (near[2], column)]
+    barrier = pltpu.get_barrier_semaphore()
+
+    def tell(sem, partners):
+        for partner in partners:
+            pl.semaphore_signal(sem, inc=1, device_id=partner, device_id_type=MESH)
+
+    tell(barrier, beside)
 
     fetches = [
         pltpu.make_async_copy(there, here, fetch_sem.at[n])
@@ -55,14 +64,6 @@
     ]
     for fetch in fetches:
         fetch.start()
-    beside = [(owner, at[1]), (owner, before), (near[0], column), (near[2], column)]
-    barrier = pltpu.get_barrier_semaphore()
-
-    def tell(sem, partners):
-        for partner in partners:
-            pl.semaphore_signal(sem, inc=1, device_id=partner, device_id_type=MESH)
-
-    tell(barrier, beside)
     pl.semaphore_wait(barrier, len(beside))
 
     step = pltpu.make_async_remote_copy(
@@ -130,6 +131,23 @@
             send(asked, tiles_ref, r, k, column, at[k])
     pack(asked, tiles_ref, 1, column, arrived, (columns + column) * ROOM)
     asked = asked_of(owner * columns + before)
+
+    step.wait_recv()
+    for k in range(half, 0, -1):
+        for r in range(3):
+            if (r, k) != (1, 1):
+                send(asked, passing, r, k, before, at[k - 1])
+    pack(asked, passing, 1, column, arrived, (columns + before) * ROOM)
+
+    reach, stage = 1, 2
+    while 2 * reach <= max(2, owners // 2):
+        far = [
+            ((owner + reach) & (owners - 1), column),
+            ((owner - reach) & (owners - 1), column),
+        ]
+        tell(ready.at[stage], far)
+        pl.semaphore_wait(ready.at[stage], 2)
+        reach, stage = 2 * reach, stage + 1
 
     nothing = 3 * columns * ROOM
     arrived[nothing] = jnp.zeros((edge, edge), BF16)
@@ -151,23 +169,6 @@
         same = source == lax.shift_right_arithmetic(entry, tile_bits)
         rank = (jnp.min(jnp.where(same, spot, FAR)) < p).astype(jnp.int32)
         place[p] = jnp.where(entry >= 0, jnp.clip(start + rank, 0, nothing), nothing)
-
-    step.wait()
-    for k in range(half, 0, -1):
-        for r in range(3):
-            if (r, k) != (1, 1):
-                send(asked, passing, r, k, before, at[k - 1])
-    pack(asked, passing, 1, column, arrived, (columns + before) * ROOM)
-
-    reach, stage = 1, 2
-    while 2 * reach <= max(2, owners // 2):
-        far = [
-            (lax.rem(owner + reach, owners), column),
-            (lax.rem(owner + owners - reach, owners), column),
-        ]
-        tell(ready.at[stage], far)
-        pl.semaphore_wait(ready.at[stage], 2)
-        reach, stage = 2 * reach, stage + 1
 
     targets = [
         [
@@ -196,7 +197,7 @@
             sent = sent + theirs.astype(jnp.int32)
 
     for copy in sends:
-        copy.wait()
+        copy.wait_recv()
 
     chem = chem_ref[...]
     inverse = 1.0 / scale_ref[...]
@@ -240,7 +241,8 @@
 
     inner = min(8, owners)
     width, depth = inner // 2, owners // inner
-    here_x, here_z = lax.div(lax.rem(owner, inner), 2), lax.div(owner, inner)
+    here_x = lax.shift_right_arithmetic(owner & (inner - 1), 1)
+    here_z = lax.shift_right_arithmetic(owner, log2(inner))
 
     def steps(*sizes):
         every = list(itertools.product(*(range(size) for size in sizes)))[1:]
@@ -251,16 +253,16 @@
             2 * columns,
             core * columns + column,
             [
-                (owner - core + lax.rem(core + dc, 2), lax.rem(column + dy, columns))
+                (owner - core + ((core + dc) & 1), (column + dy) & (columns - 1))
                 for dy, dc in steps(columns, 2)
             ],
         ),
         (
             owners // 2,
-            lax.div(owner, 2),
+            lax.shift_right_arithmetic(owner, 1),
             [
                 (
-                    lax.rem(here_z + dz, depth) * inner + lax.rem(here_x + dx, width) * 2 + core,
+                    ((here_z + dz) & (depth - 1)) * inner + ((here_x + dx) & (width - 1)) * 2 + core,
                     column,
                 )
                 for dz, dx in steps(depth, width)
@@ -337,7 +339,7 @@
             for weight, piece in zip(weights[t][1:], pieces[1:]):
                 total = total + weight * piece
             out_ref[t, pl.ds(at, 8)] = total
-    for copy in first_copies + last_copies:
+    for copy in [step, *sends, *first_copies, *last_copies]:
         copy.wait_send()
     elec_ref[...] = jnp.broadcast_to(2.0 * take(1, last_copies), elec_ref.shape)
 

time: 65.9 us -> 69 us (1.047)
  Pallas kernels: 62.3 us -> 65.5 us
    pallas_call x1, Pallas kernels: 62.3 us -> 65.5 us  [on_device(): pl.pallas_call(functools.partial(kernel, owners, columns, blocks), out_sh...]
where the time goes in v6:
time: 69 us; the launch traced here: 68.9 us
  Pallas kernels  65.5 us (95%)
  between operations  1.93 us (3%)
  local copies, waits for them, and re-layouts  1.48 us (2%)
    pallas_call x1, Pallas kernels, on_device(): pl.pallas_call(functools.partial(kernel, owners, columns, blocks), out_sh...  65.5 us

profile of v6, /device:TPU:1, one launch (start us, length us, event | category | flops | bytes accessed | tf_op | source)
XLA Modules:
  0.0 68.9 jit_solution(15870455490078855748)
XLA Ops:
  1.9 65.5 %submatrix_density.1 = (f32[16,128,128]{2,1,0:T(8,128)S(1)}, f32[8,128]{1,0:T(8,128)S(1)}) custom-call(f32[1,1]{1,0:T(1,128)} %bitcast.5.chem_ref, f32[1,1]{1,0:T(1,128)} %bitcast.6.scale_ref, bf16[16,128,128]{2,1,0:T(8,128)(2,1)} %tiles_hbm.1, s32[6,6,512]{2,1,0:T(8,128)} %bitcast.7, s32[6,512]{1,0:T(8,128)} %bitcast.8), custom_call_target="tpu_custom_call" | custom-call | tf_op jit(solution)/shard_map/submatrix_density/pallas_call | solution.py:356
  67.4 0.5 slice.3
  67.9 1.0 %copy.10 = f32[16,128,128]{2,1,0:T(8,128)} copy(f32[16,128,128]{2,1,0:T(8,128)S(1)} %get-tuple-element.8) | data formatting | bytes 2097152

commit v7 on v6

--- a/solution.py
+++ b/solution.py
@@ -131,23 +131,6 @@
             send(asked, tiles_ref, r, k, column, at[k])
     pack(asked, tiles_ref, 1, column, arrived, (columns + column) * ROOM)
     asked = asked_of(owner * columns + before)
-
-    step.wait_recv()
-    for k in range(half, 0, -1):
-        for r in range(3):
-            if (r, k) != (1, 1):
-                send(asked, passing, r, k, before, at[k - 1])
-    pack(asked, passing, 1, column, arrived, (columns + before) * ROOM)
-
-    reach, stage = 1, 2
-    while 2 * reach <= max(2, owners // 2):
-        far = [
-            ((owner + reach) & (owners - 1), column),
-            ((owner - reach) & (owners - 1), column),
-        ]
-        tell(ready.at[stage], far)
-        pl.semaphore_wait(ready.at[stage], 2)
-        reach, stage = 2 * reach, stage + 1
 
     nothing = 3 * columns * ROOM
     arrived[nothing] = jnp.zeros((edge, edge), BF16)
@@ -169,6 +152,23 @@
         same = source == lax.shift_right_arithmetic(entry, tile_bits)
         rank = (jnp.min(jnp.where(same, spot, FAR)) < p).astype(jnp.int32)
         place[p] = jnp.where(entry >= 0, jnp.clip(start + rank, 0, nothing), nothing)
+
+    step.wait_recv()
+    for k in range(half, 0, -1):
+        for r in range(3):
+            if (r, k) != (1, 1):
+                send(asked, passing, r, k, before, at[k - 1])
+    pack(asked, passing, 1, column, arrived, (columns + before) * ROOM)
+
+    reach, stage = 1, 2
+    while 2 * reach <= max(2, owners // 2):
+        far = [
+            ((owner + reach) & (owners - 1), column),
+            ((owner - reach) & (owners - 1), column),
+        ]
+        tell(ready.at[stage], far)
+        pl.semaphore_wait(ready.at[stage], 2)
+        reach, stage = 2 * reach, stage + 1
 
     targets = [
         [

time: 69 us -> 66.7 us (0.967)
  Pallas kernels: 65.5 us -> 63.1 us
    pallas_call x1, Pallas kernels: 65.5 us -> 63.1 us  [on_device(): pl.pallas_call(functools.partial(kernel, owners, columns, blocks), out_sh...]
where the time goes in v7:
time: 66.7 us; the launch traced here: 66.5 us
  Pallas kernels  63.1 us (95%)
  between operations  1.93 us (3%)
  local copies, waits for them, and re-layouts  1.48 us (2%)
    pallas_call x1, Pallas kernels, on_device(): pl.pallas_call(functools.partial(kernel, owners, columns, blocks), out_sh...  63.1 us

profile of v7, /device:TPU:1, one launch (start us, length us, event | category | flops | bytes accessed | tf_op | source)
XLA Modules:
  0.0 66.5 jit_solution(12738809770171221530)
XLA Ops:
  1.9 63.1 %submatrix_density.1 = (f32[16,128,128]{2,1,0:T(8,128)S(1)}, f32[8,128]{1,0:T(8,128)S(1)}) custom-call(f32[1,1]{1,0:T(1,128)} %bitcast.5.chem_ref, f32[1,1]{1,0:T(1,128)} %bitcast.6.scale_ref, bf16[16,128,128]{2,1,0:T(8,128)(2,1)} %tiles_hbm.1, s32[6,6,512]{2,1,0:T(8,128)} %bitcast.7, s32[6,512]{1,0:T(8,128)} %bitcast.8), custom_call_target="tpu_custom_call" | custom-call | tf_op jit(solution)/shard_map/submatrix_density/pallas_call | solution.py:356
  65.0 0.5 slice.3
  65.5 1.0 %copy.10 = f32[16,128,128]{2,1,0:T(8,128)} copy(f32[16,128,128]{2,1,0:T(8,128)S(1)} %get-tuple-element.8) | data formatting | bytes 2097152

commit v8 on v5

--- a/solution.py
+++ b/solution.py
@@ -151,23 +151,6 @@
         same = source == lax.shift_right_arithmetic(entry, tile_bits)
         rank = (jnp.min(jnp.where(same, spot, FAR)) < p).astype(jnp.int32)
         place[p] = jnp.where(entry >= 0, jnp.clip(start + rank, 0, nothing), nothing)
-
-    step.wait()
-    for k in range(half, 0, -1):
-        for r in range(3):
-            if (r, k) != (1, 1):
-                send(asked, passing, r, k, before, at[k - 1])
-    pack(asked, passing, 1, column, arrived, (columns + before) * ROOM)
-
-    reach, stage = 1, 2
-    while 2 * reach <= max(2, owners // 2):
-        far = [
-            (lax.rem(owner + reach, owners), column),
-            (lax.rem(owner + owners - reach, owners), column),
-        ]
-        tell(ready.at[stage], far)
-        pl.semaphore_wait(ready.at[stage], 2)
-        reach, stage = 2 * reach, stage + 1
 
     targets = [
         [
@@ -194,6 +177,26 @@
             for k in range(BACK):
                 chosen[r][k] = jnp.where(theirs & (sent == k), i, chosen[r][k])
             sent = sent + theirs.astype(jnp.int32)
+
+    step.wait()
+    for k in range(half, 0, -1):
+        for r in range(3):
+            if (r, k) != (1, 1):
+                send(asked, passing, r, k, before, at[k - 1])
+    pack(asked, passing, 1, column, arrived, (columns + before) * ROOM)
+
+    reaches = [1]
+    while 4 * reaches[-1] <= owners // 2:
+        reaches.append(2 * reaches[-1])
+    final = len(reaches) + 1
+    for stage, reach in enumerate(reaches, 2):
+        far = [
+            (lax.rem(owner + reach, owners), column),
+            (lax.rem(owner + owners - reach, owners), column),
+        ]
+        tell(ready.at[stage], far)
+        if stage < final:
+            pl.semaphore_wait(ready.at[stage], 2)
 
     for copy in sends:
         copy.wait()
@@ -323,7 +326,9 @@
                 )
             )
             returns[-1].start()
-    last_copies = give(1, take(0, first_copies))
+    total = take(0, first_copies)
+    pl.semaphore_wait(ready.at[final], 2)
+    last_copies = give(1, total)
     for copy in returns:
         copy.wait()
     weights = [

time: 65.9 us -> 65.9 us (level)
  no operation moved by 1% of the time
where the time goes in v8:
time: 65.9 us; the launch traced here: 65.7 us
  Pallas kernels  62.3 us (95%)
  between operations  1.93 us (3%)
  local copies, waits for them, and re-layouts  1.48 us (2%)
    pallas_call x1, Pallas kernels, on_device(): pl.pallas_call(functools.partial(kernel, owners, columns, blocks), out_sh...  62.3 us

profile of v8, /device:TPU:1, one launch (start us, length us, event | category | flops | bytes accessed | tf_op | source)
XLA Modules:
  0.0 65.7 jit_solution(2391763063454456390)
XLA Ops:
  1.9 62.3 %submatrix_density.1 = (f32[16,128,128]{2,1,0:T(8,128)S(1)}, f32[8,128]{1,0:T(8,128)S(1)}) custom-call(f32[1,1]{1,0:T(1,128)} %bitcast.5.chem_ref, f32[1,1]{1,0:T(1,128)} %bitcast.6.scale_ref, bf16[16,128,128]{2,1,0:T(8,128)(2,1)} %tiles_hbm.1, s32[6,6,512]{2,1,0:T(8,128)} %bitcast.7, s32[6,512]{1,0:T(8,128)} %bitcast.8), custom_call_target="tpu_custom_call" | custom-call | tf_op jit(solution)/shard_map/submatrix_density/pallas_call | solution.py:359
  64.3 0.5 slice.3
  64.8 1.0 %copy.10 = f32[16,128,128]{2,1,0:T(8,128)} copy(f32[16,128,128]{2,1,0:T(8,128)S(1)} %get-tuple-element.8) | data formatting | bytes 2097152

commit v9 on v4

--- a/solution.py
+++ b/solution.py
@@ -249,17 +249,17 @@
     groups = (
         (columns, column, [(owner, lax.rem(column + dy, columns)) for (dy,) in steps(columns)]),
         (
-            owners,
-            owner,
+            inner,
+            lax.rem(owner, inner),
             [
-                (
-                    lax.rem(here_z + dz, depth) * inner
-                    + lax.rem(here_x + dx, width) * 2
-                    + lax.rem(core + dc, 2),
-                    column,
-                )
-                for dz, dx, dc in steps(depth, width, 2)
+                (here_z * inner + lax.rem(here_x + dx, width) * 2 + lax.rem(core + dc, 2), column)
+                for dx, dc in steps(width, 2)
             ],
+        ),
+        (
+            depth,
+            here_z,
+            [(lax.rem(owner + dz * inner, owners), column) for (dz,) in steps(depth)],
         ),
     )
 
@@ -318,9 +318,10 @@
                 )
             )
             returns[-1].start()
-    last_copies = give(1, take(0, first_copies))
+    next_copies = give(1, take(0, first_copies))
     for copy in returns:
         copy.wait()
+    last_copies = give(2, take(1, next_copies))
     weights = [
         [jnp.where(stored[r][k] == t, 1.0, 0.0).astype(F32) for r in range(3) for k in range(BACK)]
         for t in range(tiles_per)
@@ -332,9 +333,9 @@
             for weight, piece in zip(weights[t][1:], pieces[1:]):
                 total = total + weight * piece
             out_ref[t, pl.ds(at, 8)] = total
-    for copy in first_copies + last_copies:
+    for copy in first_copies + next_copies + last_copies:
         copy.wait_send()
-    elec_ref[...] = jnp.broadcast_to(2.0 * take(1, last_copies), elec_ref.shape)
+    elec_ref[...] = jnp.broadcast_to(2.0 * take(2, last_copies), elec_ref.shape)
 
 
 def on_device(ks_tiles, chem_shift, spectral_scale, sub_tiles, result_dest):
@@ -343,7 +344,7 @@
     tiles_per, edge = ks_tiles.shape[0], ks_tiles.shape[1]
     blocks = sub_tiles.shape[1]
     order = blocks * edge
-    widest = max(columns, owners)
+    widest = max(columns, min(8, owners), owners // 8)
     vmem, smem, hbm = pltpu.VMEM, pltpu.SMEM, pl.ANY
     dma = pltpu.SemaphoreType.DMA
     density, electrons = pl.pallas_call(
@@ -367,16 +368,16 @@
             vmem((blocks + 1, edge, edge), F32),
             vmem((2, BACK, edge, edge), F32),
             vmem((3, BACK, edge, edge), F32),
-            vmem((2, 1, 128), F32),
-            vmem((2, widest, 1, 128), F32),
+            vmem((3, 1, 128), F32),
+            vmem((3, widest, 1, 128), F32),
             dma((3,)),
             dma((2,)),
             dma((3 * columns,)),
             dma((3 * columns,)),
             dma((2,)),
             dma((2,)),
-            dma((2, widest)),
-            dma((2, widest)),
+            dma((3, widest)),
+            dma((3, widest)),
             pltpu.SemaphoreType.REGULAR((2 + log2(owners),)),
         ],
         compiler_params=pltpu.CompilerParams(

time: 67.9 us -> 67.1 us (0.988)
  Pallas kernels: 64.4 us -> 63.1 us
    pallas_call x1, Pallas kernels: 64.4 us -> 63.1 us  [on_device(): pl.pallas_call(functools.partial(kernel, owners, columns, blocks), out_sh...]
where the time goes in v9:
time: 67.1 us; the launch traced here: 66.5 us
  Pallas kernels  63.1 us (94%)
  between operations  1.93 us (3%)
  local copies, waits for them, and re-layouts  1.48 us (2%)
    pallas_call x1, Pallas kernels, on_device(): pl.pallas_call(functools.partial(kernel, owners, columns, blocks), out_sh...  63.1 us

profile of v9, /device:TPU:1, one launch (start us, length us, event | category | flops | bytes accessed | tf_op | source)
XLA Modules:
  0.0 66.5 jit_solution(5366846808769870575)
XLA Ops:
  1.9 63.1 %submatrix_density.1 = (f32[16,128,128]{2,1,0:T(8,128)S(1)}, f32[8,128]{1,0:T(8,128)S(1)}) custom-call(f32[1,1]{1,0:T(1,128)} %bitcast.5.chem_ref, f32[1,1]{1,0:T(1,128)} %bitcast.6.scale_ref, bf16[16,128,128]{2,1,0:T(8,128)(2,1)} %tiles_hbm.1, s32[6,6,512]{2,1,0:T(8,128)} %bitcast.7, s32[6,512]{1,0:T(8,128)} %bitcast.8), custom_call_target="tpu_custom_call" | custom-call | tf_op jit(solution)/shard_map/submatrix_density/pallas_call | solution.py:350
  65.0 0.5 slice.3
  65.5 1.0 %copy.10 = f32[16,128,128]{2,1,0:T(8,128)} copy(f32[16,128,128]{2,1,0:T(8,128)S(1)} %get-tuple-element.8) | data formatting | bytes 2097152
